TPU v7x, 512 devices: a whole 4x4x16 slice. The times are simulated.
512 devices in a mesh: tok: 2 (over core), head: 16 (over y, x), exp: 16 (over z).
Axes of the slice: x: 4, y: 4, z: 16, core: 2. Of those that a mesh axis runs over, the one named last changes fastest.
Arguments:
- context: bfloat16 [16, 64, 4096], P('exp', 'tok', 'head'), may hold values from -6 to 6
- out_proj: bfloat16 [4096, 4096], P('head', 'exp'), may hold values from -0.125 to 0.125
- stream: float32 [16, 64, 4096], P('exp', 'tok', 'head'), may hold values from -75 to 75
- norm_gain: float32 [4096], replicated, may hold values from 0.1 to 1.9
- expert_ids: int32 [16, 64, 8], P('exp', 'tok'), may hold values from 0 to 31, as said below
- slot_ids: int32 [16, 64, 8], P('exp', 'tok'), may hold values from -1 to 11, as said below
- gate_probs: float32 [16, 64, 8], P('exp', 'tok'), may hold values from 0.02 to 0.3
- w_gate: bfloat16 [32, 3072, 4096], P(('tok', 'exp'), 'head'), may hold values from -0.09375 to 0.09375
- w_up: bfloat16 [32, 3072, 4096], P(('tok', 'exp'), 'head'), may hold values from -0.09375 to 0.09375
- w_down: bfloat16 [32, 3072, 4096], P(('tok', 'exp'), 'head'), may hold values from -0.15625 to 0.15625
Outputs:
- mixed: float32 [16, 64, 4096], P('exp', 'tok', 'head')
Inputs may be any that keep to these rules, and one draw needn't show every extreme that they name: `expert_ids`: each token names 8 different experts. `slot_ids`: within a block of 32 consecutive tokens of one image, the choices of one expert take slots 0, 1, 2, ... in token order until its 12 slots are full, later ones get -1; in every block some expert fills all 12 slots.
All inputs are finite; a program needn't handle non-finite values.
Results may differ from a plain program's by a relative error of at most 0.0034.
Values may be sent and summed in bfloat16 or wider, within the bound.
No kernel may reach another device: no remote copies, remote signals or barrier semaphores. Data moves between devices by JAX's collectives and lax.ppermute only.
A program may use at most 64 MiB of HBM per device.

v0:
```python
import jax
import jax.numpy as jnp
from jax import lax
from jax.sharding import Mesh
from jax.sharding import PartitionSpec as P

EXPERTS = 32
TOP = 8
CAP = 12
HEAD = ("head_0", "head_1")
eps_value = 1e-05


def cut_along(x, dim, count):
    shape = x.shape
    pieces = x.reshape(*shape[:dim], count, shape[dim] // count, *shape[dim + 1 :])
    return jnp.moveaxis(pieces, dim, 0)


def sum_at_owner(x, axis, dim):
    pieces = cut_along(x, dim, lax.axis_size(axis))
    arrived = lax.all_to_all(pieces, axis, split_axis=0, concat_axis=0, tiled=True)
    return arrived.astype(jnp.float32).sum(axis=0)


def over_axes(x, axes):
    for axis in axes:
        x = lax.psum(x, axis)
    return x


def gather_axes(x, axes, dim):
    result = x
    for number in range(len(axes) - 1, -1, -1):
        result = lax.all_gather(result, axes[number], axis=dim, tiled=True)
    return result


def on_device(
    context, out_proj, stream, norm_gain, expert_ids, slot_ids, gate_probs, w_gate, w_up, w_down
):
    local_context = context[0]
    own_stream = stream[0]
    col_width = own_stream.shape[1]
    full_width = col_width * lax.axis_size(HEAD)
    col_start = lax.axis_index(HEAD) * col_width
    partial_value = jnp.dot(
        local_context,
        lax.all_gather(out_proj, "exp", axis=1, tiled=True),
        preferred_element_type=jnp.float32,
    )
    resid_own = sum_at_owner(partial_value.astype(jnp.bfloat16), HEAD, 1) + own_stream
    total_sq = over_axes(jnp.sum(resid_own * resid_own, axis=1, keepdims=True), HEAD)
    gain_own = lax.dynamic_slice_in_dim(norm_gain, col_start, col_width, 0)
    normed_own = (resid_own * lax.rsqrt(total_sq / full_width + eps_value) * gain_own).astype(
        jnp.bfloat16
    )
    choice_ids = expert_ids[0]
    choice_slots = slot_ids[0]
    weights = gate_probs[0]
    spill_slot = EXPERTS * CAP
    target = jnp.where(choice_slots >= 0, choice_ids * CAP + choice_slots, spill_slot)
    outgoing = (
        jnp.zeros((spill_slot + 1, col_width), jnp.bfloat16)
        .at[target.reshape(-1)]
        .set(jnp.repeat(normed_own, TOP, axis=0))
    )
    outgoing = outgoing[:spill_slot].reshape(EXPERTS, CAP, col_width)
    tok_count = lax.axis_size("tok")
    groups = tok_count * lax.axis_size("exp")
    local_experts = w_gate.shape[0]
    arrived = lax.all_to_all(outgoing, ("tok", "exp"), split_axis=0, concat_axis=0, tiled=True)
    arrived = arrived.reshape(groups, local_experts, CAP, col_width)
    piece = gather_axes(arrived, HEAD, 3)
    gate_more = jnp.einsum("slcd,lhd->slch", piece, w_gate, preferred_element_type=jnp.float32)
    up_more = jnp.einsum("slcd,lhd->slch", piece, w_up, preferred_element_type=jnp.float32)
    hidden = (jax.nn.silu(gate_more) * up_more).astype(jnp.bfloat16)
    produced = jnp.einsum(
        "slch,lhd->slcd", hidden, w_down, preferred_element_type=jnp.float32
    ).astype(jnp.bfloat16)
    widened = lax.optimization_barrier(produced).astype(jnp.float32)
    summed = sum_at_owner(widened.astype(jnp.bfloat16), HEAD, 3)
    returned_share = lax.all_to_all(
        summed.reshape(EXPERTS, CAP, col_width).astype(jnp.bfloat16),
        ("tok", "exp"),
        split_axis=0,
        concat_axis=0,
        tiled=True,
    ).astype(jnp.float32)
    lookup_share = jnp.concatenate(
        [returned_share.reshape(spill_slot, col_width), jnp.zeros((1, col_width), jnp.float32)],
        axis=0,
    )
    picked_share = lookup_share[target]
    expert_own = jnp.sum(picked_share * weights[:, :, None], axis=1)
    return (resid_own + expert_own)[None]


def solution(mesh):
    split = Mesh(
        mesh.devices.reshape(mesh.shape["tok"], 4, 4, mesh.shape["exp"]),
        ("tok", "head_0", "head_1", "exp"),
    )
    in_specs = (
        P("exp", "tok", HEAD),
        P(HEAD, "exp"),
        P("exp", "tok", HEAD),
        P(),
        P("exp", "tok", None),
        P("exp", "tok", None),
        P("exp", "tok", None),
        P(("tok", "exp"), HEAD, None),
        P(("tok", "exp"), HEAD, None),
        P(("tok", "exp"), HEAD, None),
    )
    out_specs = P("exp", "tok", HEAD)
    return jax.shard_map(
        on_device, mesh=split, in_specs=in_specs, out_specs=out_specs, check_vma=False
    )
```

profile of v0, /device:TPU:1, one launch (start us, length us, event | category | flops | bytes accessed | tf_op | source)
XLA Modules:
  0.0 316.5 jit_solution(14243525346558986769)
XLA Ops:
  6.5 0.0 copy-start
  6.5 0.0 copy-start.4
  6.5 0.0 copy-start.3
  6.5 0.0 copy-start.1
  6.5 0.0 all-gather.5.cloned.1.call-start
  6.6 0.7 all-gather.5.cloned.1.call-update
  7.3 76.2 %all-gather.5.cloned.1.call-done = bf16[256,4096]{1,0:T(8,128)(2,1)} async-done(((bf16[256,256]{1,0:T(8,128)(2,1)}), bf16[256,4096]{1,0:T(8,128)(2,1)}) %all-gather.5.cloned.1.call-update) | async-done | bytes 2097168 | tf_op jit(solution)/shard_map/all_gather | solution.py:49
  83.5 2.1 convolution_convert_fusion.1
  85.6 0.7 copy.38
  86.3 6.5 %all-to-all-start = ((bf16[16,32,256]{2,1,0:T(8,128)(2,1)}), bf16[16,32,256]{2,1,0:T(8,128)(2,1)S(1)}, u32[]{:S(2)}, u32[]{:S(2)}) async-start(bf16[16,32,256]{2,1,0:T(8,128)(2,1)} %bitcast.101), calls=%async_computation | async-start | bytes 524288 | tf_op jit(solution)/shard_map/all_to_all | solution.py:22
  92.8 0.0 all-gather.7.cloned.1.call-start
  92.9 0.0 copy-done.4
  92.9 0.0 copy-done.3
  92.9 0.1 copy.25
  93.0 0.1 select_n.49
  93.1 0.8 dynamic_slice.3
  93.9 6.5 %all-to-all-done = bf16[16,32,256]{2,1,0:T(8,128)(2,1)S(1)} async-done(((bf16[16,32,256]{2,1,0:T(8,128)(2,1)}), bf16[16,32,256]{2,1,0:T(8,128)(2,1)S(1)}, u32[]{:S(2)}, u32[]{:S(2)}) %all-to-all-start) | async-done | bytes 262176 | tf_op jit(solution)/shard_map/all_to_all | solution.py:22
  100.4 0.0 copy-done.1
  100.4 0.1 multiply_reduce_fusion
  100.5 6.6 %psum.14 = f32[32,1]{0,1:T(1,128)S(1)} all-reduce(f32[32,1]{0,1:T(1,128)S(1)} %bitcast.107), channel_id=1, replica_groups=mesh['tok'=2,'head_0'=4,'head_1'=4,'exp'=16] {'head_0'}, use_global_device_ids=true, to_apply=%region_2.0 | all-reduce | flops 32 | bytes 256 | tf_op jit(solution)/shard_map/psum | solution.py:28
  107.1 7.0 %psum.15 = f32[32,1]{0,1:T(1,128)S(1)} all-reduce(f32[32,1]{0,1:T(1,128)S(1)} %psum.14), channel_id=1, replica_groups=mesh['tok'=2,'head_0'=4,'head_1'=4,'exp'=16] {'head_1'}, use_global_device_ids=true, to_apply=%region_3.0 | all-reduce | flops 32 | bytes 256 | tf_op jit(solution)/shard_map/psum | solution.py:28
  114.1 0.1 multiply_convert_fusion
  114.2 1.5 scatter_custom_fusion
  115.8 0.0 copy-start.5
  115.8 44.8 %all_to_all.20 = bf16[32,12,256]{2,1,0:T(8,128)(2,1)S(1)} all-to-all(bf16[32,12,256]{2,1,0:T(8,128)(2,1)S(1)} %reshape.147), channel_id=1, replica_groups=mesh['tok'=2,'head_0'=4,'head_1'=4,'exp'=16] {'tok','exp'}, dimensions={0} | all-to-all | bytes 393216 | tf_op jit(solution)/shard_map/all_to_all | solution.py:72
  160.6 0.1 copy.26
  160.6 13.4 %all-gather = bf16[32,12,1024]{2,0,1:T(8,128)(2,1)} all-gather(bf16[32,12,256]{2,0,1:T(8,128)(2,1)S(1)} %copy.26), channel_id=2, replica_groups=mesh['tok'=2,'head_0'=4,'head_1'=4,'exp'=16] {'head_1'}, dimensions={2}, use_global_device_ids=true | all-gather | bytes 983040 | tf_op jit(solution)/shard_map/all_gather | solution.py:35
  174.0 0.0 all-gather.7.cloned.1.call-update
  174.0 36.9 %all-gather.7.cloned.1.call-done = bf16[32,12,4096]{2,0,1:T(8,128)(2,1)} async-done(((bf16[32,12,1024]{2,0,1:T(8,128)(2,1)}), bf16[32,12,4096]{2,0,1:T(8,128)(2,1)}) %all-gather.7.cloned.1.call-update) | async-done | bytes 3145744 | tf_op jit(solution)/shard_map/all_gather | solution.py:35
  210.9 0.0 copy-done.5
  210.9 3.7 %fusion.6 = f32[32,1,12,192]{3,0,2,1:T(8,128)} fusion(bf16[32,12,4096]{2,0,1:T(8,128)(2,1)} %all-gather.7.cloned.1.call-done, bf16[1,192,4096]{2,1,0:T(8,128)(2,1)S(1)} %copy-done.5), kind=kOutput, calls=%fused_computation.11 | convolution fusion | flops 603979776 | bytes 5013504 | tf_op jit(solution)/shard_map/slcd,lhd->slch/dot_general | solution.py:75
  214.6 0.0 copy-done
  214.6 7.6 %fusion = bf16[32,1,12,4096]{3,0,2,1:T(8,128)(2,1)} fusion(bf16[1,192,4096]{2,1,0:T(8,128)(2,1)S(1)} %copy-done, bf16[32,12,4096]{2,0,1:T(8,128)(2,1)} %all-gather.7.cloned.1.call-done, bf16[1,192,4096]{2,1,0:T(8,128)(2,1)} %param.18, f32[32,1,12,192]{3,0,2,1:T(8,128)} %fusion.6), kind=kOutput, calls=%fused_computation.3 | convolution fusion | flops 1209974784 | bytes 9732096 | tf_op jit(solution)/shard_map/slch,lhd->slcd/dot_general | solution.py:78
  222.2 2.3 copy.37
  224.5 44.0 %all_to_all.21 = bf16[16,32,1,12,256]{4,1,3,2,0:T(8,128)(2,1)} all-to-all(bf16[16,32,1,12,256]{4,1,3,2,0:T(8,128)(2,1)S(1)} %bitcast.102), channel_id=1, replica_groups=mesh['tok'=2,'head_0'=4,'head_1'=4,'exp'=16] {'head_0','head_1'}, dimensions={0} | all-to-all | bytes 6291456 | tf_op jit(solution)/shard_map/all_to_all | solution.py:22
  268.5 0.0 copy-start.2
  268.5 2.6 reduce_sum.46
  271.0 0.8 copy.29
  271.8 14.3 %all-to-all-start.3 = ((bf16[32,12,256]{2,1,0:T(8,128)(2,1)}), bf16[32,12,256]{2,1,0:T(8,128)(2,1)S(1)}, u32[]{:S(2)}, u32[]{:S(2)}) async-start(bf16[32,12,256]{2,1,0:T(8,128)(2,1)} %copy.29), calls=%async_computation.3 | async-start | bytes 524288 | tf_op jit(solution)/shard_map/all_to_all | solution.py:83
  286.2 0.1 copy.30
  286.2 0.1 reshape.158
  286.3 0.0 copy-done.2
  286.3 0.1 copy.31
  286.4 21.4 %all-to-all-done.3 = bf16[32,12,256]{2,1,0:T(8,128)(2,1)S(1)} async-done(((bf16[32,12,256]{2,1,0:T(8,128)(2,1)}), bf16[32,12,256]{2,1,0:T(8,128)(2,1)S(1)}, u32[]{:S(2)}, u32[]{:S(2)}) %all-to-all-start.3) | async-done | bytes 196640 | tf_op jit(solution)/shard_map/all_to_all | solution.py:83
  307.9 1.0 gather_fusion
  308.9 0.1 fusion.28
  309.0 0.6 bitcast_add_fusion
  (9 shorter events, 0.2 us)
Async XLA Ops:
  6.5 208.1 %copy-start = (bf16[1,192,4096]{2,1,0:T(8,128)(2,1)S(1)}, bf16[1,192,4096]{2,1,0:T(8,128)(2,1)}, u32[]{:S(2)}) copy-start(bf16[1,192,4096]{2,1,0:T(8,128)(2,1)} %param.19) | copy-start | bytes 4718596
  6.5 86.4 %copy-start.4 = (s32[1,32,8]{1,2,0:T(8,128)S(1)}, s32[1,32,8]{1,2,0:T(8,128)}, u32[]{:S(2)}) copy-start(s32[1,32,8]{1,2,0:T(8,128)} %param.14) | copy-start | bytes 3076
  6.5 86.4 %copy-start.3 = (s32[1,32,8]{1,2,0:T(8,128)S(1)}, s32[1,32,8]{1,2,0:T(8,128)}, u32[]{:S(2)}) copy-start(s32[1,32,8]{1,2,0:T(8,128)} %param.15) | copy-start | bytes 3076
  6.5 93.9 %copy-start.1 = (f32[1,32,256]{2,1,0:T(8,128)S(1)}, f32[1,32,256]{2,1,0:T(8,128)}, u32[]{:S(2)}) copy-start(f32[1,32,256]{2,1,0:T(8,128)} %param.12) | copy-start | bytes 98308
  6.5 77.0 %all-gather.5.cloned.1.call-start = ((), (), s32[]{:S(2)}) async-start(), calls=%async_computation.4 | async-start | bytes 2228224 | tf_op jit(solution)/shard_map/all_gather | solution.py:49
  86.3 14.1 %all-to-all-start = ((bf16[16,32,256]{2,1,0:T(8,128)(2,1)}), bf16[16,32,256]{2,1,0:T(8,128)(2,1)S(1)}, u32[]{:S(2)}, u32[]{:S(2)}) async-start(bf16[16,32,256]{2,1,0:T(8,128)(2,1)} %bitcast.101), calls=%async_computation | async-start | bytes 524288 | tf_op jit(solution)/shard_map/all_to_all | solution.py:22
  92.8 118.1 %all-gather.7.cloned.1.call-start = ((), (), s32[]{:S(2)}) async-start(), calls=%async_computation.5 | async-start | bytes 3932160 | tf_op jit(solution)/shard_map/all_gather | solution.py:35
  115.8 95.2 %copy-start.5 = (bf16[1,192,4096]{2,1,0:T(8,128)(2,1)S(1)}, bf16[1,192,4096]{2,1,0:T(8,128)(2,1)}, u32[]{:S(2)}) copy-start(bf16[1,192,4096]{2,1,0:T(8,128)(2,1)} %param.17) | copy-start | bytes 4718596
  268.5 17.9 %copy-start.2 = (f32[1,32,8]{1,2,0:T(8,128)S(1)}, f32[1,32,8]{1,2,0:T(8,128)}, u32[]{:S(2)}) copy-start(f32[1,32,8]{1,2,0:T(8,128)} %param.16) | copy-start | bytes 3076
  271.8 36.0 %all-to-all-start.3 = ((bf16[32,12,256]{2,1,0:T(8,128)(2,1)}), bf16[32,12,256]{2,1,0:T(8,128)(2,1)S(1)}, u32[]{:S(2)}, u32[]{:S(2)}) async-start(bf16[32,12,256]{2,1,0:T(8,128)(2,1)} %copy.29), calls=%async_computation.3 | async-start | bytes 524288 | tf_op jit(solution)/shard_map/all_to_all | solution.py:83
Sparse Core Ops, SparseCore 0:
  9.4 74.0 all-gather.4
  174.2 36.7 all-gather.6
where the time goes:
time: 317 us; the launch traced here: 316 us
  waiting for transfers between devices  142 us (45%)
  blocking collectives  116 us (37%)
  starting transfers between devices  20.9 us (7%)
  between operations  13.6 us (4%)
  matrix products  13.3 us (4%)
  local copies, waits for them, and re-layouts  7.68 us (2%)
  other arithmetic  3.61 us (1%)
    all_gather x1, waiting for transfers between devices, on_device(): lax.all_gather(out_proj, 'exp', axis=1, tiled=True)  76.2 us
    all_to_all x1, blocking collectives, on_device(): lax.all_to_all(outgoing, ('tok', 'exp'), split_axis=0, concat_axis=0, til...  44.8 us
    all_to_all x1, blocking collectives, sum_at_owner(): lax.all_to_all(pieces, axis, split_axis=0, concat_axis=0, tiled=True)  44 us
    all_gather x1, waiting for transfers between devices, gather_axes(): result = lax.all_gather(result, axes[number], axis=dim, tiled=True)  36.9 us
    all_to_all x1, waiting for transfers between devices, on_device(): lax.all_to_all(summed.reshape(EXPERTS, CAP, col_width).astype(jnp.bfloat1...  21.4 us
    all_to_all x1, starting transfers between devices, on_device(): lax.all_to_all(summed.reshape(EXPERTS, CAP, col_width).astype(jnp.bfloat1...  14.3 us
    psum x2, blocking collectives, over_axes(): x = lax.psum(x, axis)  13.5 us
    all_gather x1, blocking collectives, gather_axes(): result = lax.all_gather(result, axes[number], axis=dim, tiled=True)  13.4 us
  transfers between devices with their start and end apart: 4, of which 4 were waited for; matrix products, arithmetic and copies ran while one was open for 0% of the time, Pallas kernels for 0%

commit v1 on v0

--- a/solution.py
+++ b/solution.py
@@ -9,6 +9,24 @@
 CAP = 12
 HEAD = ("head_0", "head_1")
 eps_value = 1e-05
+
+
+def ring_gather(value, axis, dim):
+    ways, here, step = (lax.axis_size(axis), lax.axis_index(axis), value.shape[dim])
+    lengths = [n * ways if d == dim else n for d, n in enumerate(value.shape)]
+    full = lax.dynamic_update_slice_in_dim(
+        jnp.zeros(lengths, value.dtype), value, here * step, axis=dim
+    )
+    going_up = going_down = value
+    for far in range(1, ways // 2 + 1):
+        going_up = lax.ppermute(going_up, axis, [(d, (d + 1) % ways) for d in range(ways)])
+        full = lax.dynamic_update_slice_in_dim(full, going_up, (here - far) % ways * step, axis=dim)
+        if 2 * far < ways:
+            going_down = lax.ppermute(going_down, axis, [(d, (d - 1) % ways) for d in range(ways)])
+            full = lax.dynamic_update_slice_in_dim(
+                full, going_down, (here + far) % ways * step, axis=dim
+            )
+    return full
 
 
 def cut_along(x, dim, count):
@@ -45,9 +63,7 @@
     full_width = col_width * lax.axis_size(HEAD)
     col_start = lax.axis_index(HEAD) * col_width
     partial_value = jnp.dot(
-        local_context,
-        lax.all_gather(out_proj, "exp", axis=1, tiled=True),
-        preferred_element_type=jnp.float32,
+        local_context, ring_gather(out_proj, "exp", 1), preferred_element_type=jnp.float32
     )
     resid_own = sum_at_owner(partial_value.astype(jnp.bfloat16), HEAD, 1) + own_stream
     total_sq = over_axes(jnp.sum(resid_own * resid_own, axis=1, keepdims=True), HEAD)

time: 317 us -> 305 us (0.962)
  waiting for transfers between devices: 142 us -> 74.7 us
  starting transfers between devices: 20.9 us -> 75.9 us
    all_gather x1 -> x0, waiting for transfers between devices: 76.2 us -> none  [on_device(): lax.all_gather(out_proj, 'exp', axis=1, tiled=True)]
    ppermute x0 -> x15, starting transfers between devices: none -> 54.8 us  [the longest x7 36.9 us: ring_gather(): lax.ppermute(going_down, axis, [(d, (d - 1) % ways) for d in range(ways)])]
    ppermute x0 -> x15, waiting for transfers between devices: none -> 9.87 us  [the longest x8 9.85 us: ring_gather(): lax.ppermute(going_up, axis, [(d, (d + 1) % ways) for d in range(ways)])]
  transfers between devices with their start and end apart: 4 -> 18, of which waited for: 4 -> 11; matrix products, arithmetic and copies ran while one was open for 0% -> 1% of each run, Pallas kernels for 0% -> 0%
where the time goes in v1:
time: 305 us; the launch traced here: 304 us
  blocking collectives  115 us (38%)
  starting transfers between devices  75.9 us (25%)
  waiting for transfers between devices  74.7 us (24%)
  between operations  14.2 us (5%)
  matrix products  11.6 us (4%)
  local copies, waits for them, and re-layouts  8.21 us (3%)
  other arithmetic  3.61 us (1%)
    all_to_all x1, blocking collectives, on_device(): lax.all_to_all(outgoing, ('tok', 'exp'), split_axis=0, concat_axis=0, til...  44.5 us
    all_to_all x1, blocking collectives, sum_at_owner(): lax.all_to_all(pieces, axis, split_axis=0, concat_axis=0, tiled=True)  44 us
    ppermute x7, starting transfers between devices, ring_gather(): lax.ppermute(going_down, axis, [(d, (d - 1) % ways) for d in range(ways)])  36.9 us
    all_gather x1, waiting for transfers between devices, gather_axes(): result = lax.all_gather(result, axes[number], axis=dim, tiled=True)  36.9 us
    all_to_all x1, waiting for transfers between devices, on_device(): lax.all_to_all(summed.reshape(EXPERTS, CAP, col_width).astype(jnp.bfloat1...  21.4 us
    ppermute x8, starting transfers between devices, ring_gather(): lax.ppermute(going_up, axis, [(d, (d + 1) % ways) for d in range(ways)])  17.9 us
    all_to_all x1, starting transfers between devices, on_device(): lax.all_to_all(summed.reshape(EXPERTS, CAP, col_width).astype(jnp.bfloat1...  14.3 us
    psum x2, blocking collectives, over_axes(): x = lax.psum(x, axis)  13.5 us
  transfers between devices with their start and end apart: 18, of which 11 were waited for; matrix products, arithmetic and copies ran while one was open for 1% of the time, Pallas kernels for 0%

profile of v1, /device:TPU:1, one launch (start us, length us, event | category | flops | bytes accessed | tf_op | source)
XLA Modules:
  0.0 303.7 jit_solution(3841631389184500405)
XLA Ops:
  6.5 4.5 %collective-permute-start = (bf16[256,256]{1,0:T(8,128)(2,1)}, bf16[256,256]{1,0:T(8,128)(2,1)S(1)}, u32[]{:S(2)}, u32[]{:S(2)}) collective-permute-start(bf16[256,256]{1,0:T(8,128)(2,1)} %param.11), channel_id=1, source_target_pairs={{0,1},{1,2},{2,3},{3,4},{4,5},{5,6},{6,7},{7,8},{8,9},{9,10},{10,1... | collective-permute-start | bytes 393224 | tf_op jit(solution)/shard_map/ppermute | solution.py:22
  11.0 9.5 %collective-permute-start.1 = (bf16[256,256]{1,0:T(8,128)(2,1)}, bf16[256,256]{1,0:T(8,128)(2,1)S(1)}, u32[]{:S(2)}, u32[]{:S(2)}) collective-permute-start(bf16[256,256]{1,0:T(8,128)(2,1)} %param.11), channel_id=1, source_target_pairs={{0,15},{1,0},{2,1},{3,2},{4,3},{5,4},{6,5},{7,6},{8,7},{9,8},{10,9... | collective-permute-start | bytes 393224 | tf_op jit(solution)/shard_map/ppermute | solution.py:25
  20.9 0.2 broadcast_in_dim.21
  21.1 0.9 collective-permute-done
  22.0 1.9 collective-permute-start.2
  24.0 4.6 %collective-permute-start.3 = (bf16[256,256]{1,0:T(8,128)(2,1)S(1)}, bf16[256,256]{1,0:T(8,128)(2,1)S(1)}, u32[]{:S(2)}, u32[]{:S(2)}) collective-permute-start(bf16[256,256]{1,0:T(8,128)(2,1)S(1)} %collective-permute-done.1), channel_id=1, source_target_pairs={{0,15},{1,0},{2,1},{3,2},{4,3},{5,4},{6,5},{7,6},{8,7},{9,8},{10,9... | collective-permute-start | bytes 393224 | tf_op jit(solution)/shard_map/ppermute | solution.py:25
  28.6 0.4 collective-permute-done.2
  28.9 1.9 collective-permute-start.4
  30.9 4.6 %collective-permute-start.5 = (bf16[256,256]{1,0:T(8,128)(2,1)S(1)}, bf16[256,256]{1,0:T(8,128)(2,1)S(1)}, u32[]{:S(2)}, u32[]{:S(2)}) collective-permute-start(bf16[256,256]{1,0:T(8,128)(2,1)S(1)} %collective-permute-done.3), channel_id=1, source_target_pairs={{0,15},{1,0},{2,1},{3,2},{4,3},{5,4},{6,5},{7,6},{8,7},{9,8},{10,9... | collective-permute-start | bytes 393224 | tf_op jit(solution)/shard_map/ppermute | solution.py:25
  35.5 0.4 collective-permute-done.4
  35.9 1.9 collective-permute-start.6
  37.8 4.6 %collective-permute-start.7 = (bf16[256,256]{1,0:T(8,128)(2,1)S(1)}, bf16[256,256]{1,0:T(8,128)(2,1)S(1)}, u32[]{:S(2)}, u32[]{:S(2)}) collective-permute-start(bf16[256,256]{1,0:T(8,128)(2,1)S(1)} %collective-permute-done.5), channel_id=1, source_target_pairs={{0,15},{1,0},{2,1},{3,2},{4,3},{5,4},{6,5},{7,6},{8,7},{9,8},{10,9... | collective-permute-start | bytes 393224 | tf_op jit(solution)/shard_map/ppermute | solution.py:25
  42.4 0.4 collective-permute-done.6
  42.8 1.9 collective-permute-start.8
  44.7 4.6 %collective-permute-start.9 = (bf16[256,256]{1,0:T(8,128)(2,1)S(1)}, bf16[256,256]{1,0:T(8,128)(2,1)S(1)}, u32[]{:S(2)}, u32[]{:S(2)}) collective-permute-start(bf16[256,256]{1,0:T(8,128)(2,1)S(1)} %collective-permute-done.7), channel_id=1, source_target_pairs={{0,15},{1,0},{2,1},{3,2},{4,3},{5,4},{6,5},{7,6},{8,7},{9,8},{10,9... | collective-permute-start | bytes 393224 | tf_op jit(solution)/shard_map/ppermute | solution.py:25
  49.3 0.4 collective-permute-done.8
  49.7 1.9 collective-permute-start.10
  51.6 4.6 %collective-permute-start.11 = (bf16[256,256]{1,0:T(8,128)(2,1)S(1)}, bf16[256,256]{1,0:T(8,128)(2,1)S(1)}, u32[]{:S(2)}, u32[]{:S(2)}) collective-permute-start(bf16[256,256]{1,0:T(8,128)(2,1)S(1)} %collective-permute-done.9), channel_id=1, source_target_pairs={{0,15},{1,0},{2,1},{3,2},{4,3},{5,4},{6,5},{7,6},{8,7},{9,8},{10,9... | collective-permute-start | bytes 393224 | tf_op jit(solution)/shard_map/ppermute | solution.py:25
  56.2 0.4 collective-permute-done.10
  56.6 1.9 collective-permute-start.12
  58.5 4.6 %collective-permute-start.13 = (bf16[256,256]{1,0:T(8,128)(2,1)S(1)}, bf16[256,256]{1,0:T(8,128)(2,1)S(1)}, u32[]{:S(2)}, u32[]{:S(2)}) collective-permute-start(bf16[256,256]{1,0:T(8,128)(2,1)S(1)} %collective-permute-done.11), channel_id=1, source_target_pairs={{0,15},{1,0},{2,1},{3,2},{4,3},{5,4},{6,5},{7,6},{8,7},{9,8},{10,9... | collective-permute-start | bytes 393224 | tf_op jit(solution)/shard_map/ppermute | solution.py:25
  63.2 1.1 collective-permute-done.12
  64.3 1.9 collective-permute-start.14
  66.3 6.1 %collective-permute-done.14 = bf16[256,256]{1,0:T(8,128)(2,1)S(1)} collective-permute-done((bf16[256,256]{1,0:T(8,128)(2,1)S(1)}, bf16[256,256]{1,0:T(8,128)(2,1)S(1)}, u32[]{:S(2)}, u32[]{:S(2)}) %collective-permute-start.14) | collective-permute-done | bytes 131104 | tf_op jit(solution)/shard_map/ppermute | solution.py:22
  72.4 0.5 convolution_convert_fusion.1
  72.8 0.7 copy.38
  73.6 6.8 %all-to-all-start = ((bf16[16,32,256]{2,1,0:T(8,128)(2,1)}), bf16[16,32,256]{2,1,0:T(8,128)(2,1)S(1)}, u32[]{:S(2)}, u32[]{:S(2)}) async-start(bf16[16,32,256]{2,1,0:T(8,128)(2,1)} %bitcast.102), calls=%async_computation | async-start | bytes 524288 | tf_op jit(solution)/shard_map/all_to_all | solution.py:40
  80.5 0.1 select_n.191
  80.6 0.8 dynamic_slice.3
  81.4 6.5 %all-to-all-done = bf16[16,32,256]{2,1,0:T(8,128)(2,1)S(1)} async-done(((bf16[16,32,256]{2,1,0:T(8,128)(2,1)}), bf16[16,32,256]{2,1,0:T(8,128)(2,1)S(1)}, u32[]{:S(2)}, u32[]{:S(2)}) %all-to-all-start) | async-done | bytes 262176 | tf_op jit(solution)/shard_map/all_to_all | solution.py:40
  87.9 0.1 multiply_reduce_fusion
  88.1 7.2 %psum.14 = f32[32,1]{0,1:T(1,128)S(1)} all-reduce(f32[32,1]{0,1:T(1,128)S(1)} %bitcast.108), channel_id=1, replica_groups=mesh['tok'=2,'head_0'=4,'head_1'=4,'exp'=16] {'head_0'}, use_global_device_ids=true, to_apply=%region_2.3 | all-reduce | flops 32 | bytes 256 | tf_op jit(solution)/shard_map/psum | solution.py:46
  95.3 6.3 %psum.15 = f32[32,1]{0,1:T(1,128)S(1)} all-reduce(f32[32,1]{0,1:T(1,128)S(1)} %psum.14), channel_id=1, replica_groups=mesh['tok'=2,'head_0'=4,'head_1'=4,'exp'=16] {'head_1'}, use_global_device_ids=true, to_apply=%region_3.4 | all-reduce | flops 32 | bytes 256 | tf_op jit(solution)/shard_map/psum | solution.py:46
  101.7 1.5 scatter_custom_fusion
  103.3 44.5 %all_to_all.20 = bf16[32,12,256]{2,1,0:T(8,128)(2,1)S(1)} all-to-all(bf16[32,12,256]{2,1,0:T(8,128)(2,1)S(1)} %reshape.147), channel_id=1, replica_groups=mesh['tok'=2,'head_0'=4,'head_1'=4,'exp'=16] {'tok','exp'}, dimensions={0} | all-to-all | bytes 393216 | tf_op jit(solution)/shard_map/all_to_all | solution.py:88
  147.8 13.4 %all-gather = bf16[32,12,1024]{2,0,1:T(8,128)(2,1)} all-gather(bf16[32,12,256]{2,0,1:T(8,128)(2,1)S(1)} %copy.26), channel_id=2, replica_groups=mesh['tok'=2,'head_0'=4,'head_1'=4,'exp'=16] {'head_1'}, dimensions={2}, use_global_device_ids=true | all-gather | bytes 983040 | tf_op jit(solution)/shard_map/all_gather | solution.py:53
  161.2 36.9 %all-gather.4.cloned.1.call-done = bf16[32,12,4096]{2,0,1:T(8,128)(2,1)} async-done(((bf16[32,12,1024]{2,0,1:T(8,128)(2,1)}), bf16[32,12,4096]{2,0,1:T(8,128)(2,1)}) %all-gather.4.cloned.1.call-update) | async-done | bytes 3145744 | tf_op jit(solution)/shard_map/all_gather | solution.py:53
  198.1 3.6 %fusion.6 = f32[32,1,12,192]{3,0,2,1:T(8,128)} fusion(bf16[32,12,4096]{2,0,1:T(8,128)(2,1)} %all-gather.4.cloned.1.call-done, bf16[1,192,4096]{2,1,0:T(8,128)(2,1)S(1)} %copy-done.7), kind=kOutput, calls=%fused_computation.11 | convolution fusion | flops 603979776 | bytes 5013504 | tf_op jit(solution)/shard_map/slcd,lhd->slch/dot_general | solution.py:91
  201.8 7.5 %fusion = bf16[32,1,12,4096]{3,0,2,1:T(8,128)(2,1)} fusion(bf16[1,192,4096]{2,1,0:T(8,128)(2,1)S(1)} %copy-done, bf16[32,12,4096]{2,0,1:T(8,128)(2,1)} %all-gather.4.cloned.1.call-done, bf16[1,192,4096]{2,1,0:T(8,128)(2,1)} %param.18, f32[32,1,12,192]{3,0,2,1:T(8,128)} %fusion.6), kind=kOutput, calls=%fused_computation.3 | convolution fusion | flops 1209974784 | bytes 9732096 | tf_op jit(solution)/shard_map/slch,lhd->slcd/dot_general | solution.py:94
  209.3 2.3 copy.37
  211.6 44.0 %all_to_all.21 = bf16[16,32,1,12,256]{4,1,3,2,0:T(8,128)(2,1)} all-to-all(bf16[16,32,1,12,256]{4,1,3,2,0:T(8,128)(2,1)S(1)} %bitcast.103), channel_id=1, replica_groups=mesh['tok'=2,'head_0'=4,'head_1'=4,'exp'=16] {'head_0','head_1'}, dimensions={0} | all-to-all | bytes 6291456 | tf_op jit(solution)/shard_map/all_to_all | solution.py:40
  255.6 2.6 reduce_sum.46
  258.2 0.8 copy.29
  259.0 14.3 %all-to-all-start.3 = ((bf16[32,12,256]{2,1,0:T(8,128)(2,1)}), bf16[32,12,256]{2,1,0:T(8,128)(2,1)S(1)}, u32[]{:S(2)}, u32[]{:S(2)}) async-start(bf16[32,12,256]{2,1,0:T(8,128)(2,1)} %copy.29), calls=%async_computation.3 | async-start | bytes 524288 | tf_op jit(solution)/shard_map/all_to_all | solution.py:99
  273.6 21.4 %all-to-all-done.3 = bf16[32,12,256]{2,1,0:T(8,128)(2,1)S(1)} async-done(((bf16[32,12,256]{2,1,0:T(8,128)(2,1)}), bf16[32,12,256]{2,1,0:T(8,128)(2,1)S(1)}, u32[]{:S(2)}, u32[]{:S(2)}) %all-to-all-start.3) | async-done | bytes 196640 | tf_op jit(solution)/shard_map/all_to_all | solution.py:99
  295.1 1.0 gather_fusion
  296.1 0.1 fusion.28
  296.2 0.6 bitcast_add_fusion
  (56 shorter events, 1.0 us)
Async XLA Ops:
  6.5 195.2 %copy-start = (bf16[1,192,4096]{2,1,0:T(8,128)(2,1)S(1)}, bf16[1,192,4096]{2,1,0:T(8,128)(2,1)}, u32[]{:S(2)}) copy-start(bf16[1,192,4096]{2,1,0:T(8,128)(2,1)} %param.19) | copy-start | bytes 4718596
  6.5 14.6 %copy-start.2 = (bf16[256,256]{1,0:T(8,128)(2,1)S(1)}, bf16[256,256]{1,0:T(8,128)(2,1)}, u32[]{:S(2)}) copy-start(bf16[256,256]{1,0:T(8,128)(2,1)} %param.11) | copy-start | bytes 393220
  6.5 15.5 %collective-permute-start = (bf16[256,256]{1,0:T(8,128)(2,1)}, bf16[256,256]{1,0:T(8,128)(2,1)S(1)}, u32[]{:S(2)}, u32[]{:S(2)}) collective-permute-start(bf16[256,256]{1,0:T(8,128)(2,1)} %param.11), channel_id=1, source_target_pairs={{0,1},{1,2},{2,3},{3,4},{4,5},{5,6},{6,7},{7,8},{8,9},{9,10},{10,1... | collective-permute-start | bytes 393224 | tf_op jit(solution)/shard_map/ppermute | solution.py:22
  11.0 12.9 %collective-permute-start.1 = (bf16[256,256]{1,0:T(8,128)(2,1)}, bf16[256,256]{1,0:T(8,128)(2,1)S(1)}, u32[]{:S(2)}, u32[]{:S(2)}) collective-permute-start(bf16[256,256]{1,0:T(8,128)(2,1)} %param.11), channel_id=1, source_target_pairs={{0,15},{1,0},{2,1},{3,2},{4,3},{5,4},{6,5},{7,6},{8,7},{9,8},{10,9... | collective-permute-start | bytes 393224 | tf_op jit(solution)/shard_map/ppermute | solution.py:25
  21.1 51.3 %copy-start.3 = (bf16[1,32,256]{2,1,0:T(8,128)(2,1)S(1)}, bf16[1,32,256]{2,1,0:T(8,128)(2,1)}, u32[]{:S(2)}) copy-start(bf16[1,32,256]{2,1,0:T(8,128)(2,1)} %param.10) | copy-start | bytes 49156
  22.0 6.9 %collective-permute-start.2 = (bf16[256,256]{1,0:T(8,128)(2,1)S(1)}, bf16[256,256]{1,0:T(8,128)(2,1)S(1)}, u32[]{:S(2)}, u32[]{:S(2)}) collective-permute-start(bf16[256,256]{1,0:T(8,128)(2,1)S(1)} %collective-permute-done), channel_id=1, source_target_pairs={{0,1},{1,2},{2,3},{3,4},{4,5},{5,6},{6,7},{7,8},{8,9},{9,10},{10,1... | collective-permute-start | bytes 393224 | tf_op jit(solution)/shard_map/ppermute | solution.py:22
  24.0 6.9 %collective-permute-start.3 = (bf16[256,256]{1,0:T(8,128)(2,1)S(1)}, bf16[256,256]{1,0:T(8,128)(2,1)S(1)}, u32[]{:S(2)}, u32[]{:S(2)}) collective-permute-start(bf16[256,256]{1,0:T(8,128)(2,1)S(1)} %collective-permute-done.1), channel_id=1, source_target_pairs={{0,15},{1,0},{2,1},{3,2},{4,3},{5,4},{6,5},{7,6},{8,7},{9,8},{10,9... | collective-permute-start | bytes 393224 | tf_op jit(solution)/shard_map/ppermute | solution.py:25
  28.9 6.9 %collective-permute-start.4 = (bf16[256,256]{1,0:T(8,128)(2,1)S(1)}, bf16[256,256]{1,0:T(8,128)(2,1)S(1)}, u32[]{:S(2)}, u32[]{:S(2)}) collective-permute-start(bf16[256,256]{1,0:T(8,128)(2,1)S(1)} %collective-permute-done.2), channel_id=1, source_target_pairs={{0,1},{1,2},{2,3},{3,4},{4,5},{5,6},{6,7},{7,8},{8,9},{9,10},{10,1... | collective-permute-start | bytes 393224 | tf_op jit(solution)/shard_map/ppermute | solution.py:22
  30.9 6.9 %collective-permute-start.5 = (bf16[256,256]{1,0:T(8,128)(2,1)S(1)}, bf16[256,256]{1,0:T(8,128)(2,1)S(1)}, u32[]{:S(2)}, u32[]{:S(2)}) collective-permute-start(bf16[256,256]{1,0:T(8,128)(2,1)S(1)} %collective-permute-done.3), channel_id=1, source_target_pairs={{0,15},{1,0},{2,1},{3,2},{4,3},{5,4},{6,5},{7,6},{8,7},{9,8},{10,9... | collective-permute-start | bytes 393224 | tf_op jit(solution)/shard_map/ppermute | solution.py:25
  35.9 6.9 %collective-permute-start.6 = (bf16[256,256]{1,0:T(8,128)(2,1)S(1)}, bf16[256,256]{1,0:T(8,128)(2,1)S(1)}, u32[]{:S(2)}, u32[]{:S(2)}) collective-permute-start(bf16[256,256]{1,0:T(8,128)(2,1)S(1)} %collective-permute-done.4), channel_id=1, source_target_pairs={{0,1},{1,2},{2,3},{3,4},{4,5},{5,6},{6,7},{7,8},{8,9},{9,10},{10,1... | collective-permute-start | bytes 393224 | tf_op jit(solution)/shard_map/ppermute | solution.py:22
  37.8 6.9 %collective-permute-start.7 = (bf16[256,256]{1,0:T(8,128)(2,1)S(1)}, bf16[256,256]{1,0:T(8,128)(2,1)S(1)}, u32[]{:S(2)}, u32[]{:S(2)}) collective-permute-start(bf16[256,256]{1,0:T(8,128)(2,1)S(1)} %collective-permute-done.5), channel_id=1, source_target_pairs={{0,15},{1,0},{2,1},{3,2},{4,3},{5,4},{6,5},{7,6},{8,7},{9,8},{10,9... | collective-permute-start | bytes 393224 | tf_op jit(solution)/shard_map/ppermute | solution.py:25
  42.8 6.9 %collective-permute-start.8 = (bf16[256,256]{1,0:T(8,128)(2,1)S(1)}, bf16[256,256]{1,0:T(8,128)(2,1)S(1)}, u32[]{:S(2)}, u32[]{:S(2)}) collective-permute-start(bf16[256,256]{1,0:T(8,128)(2,1)S(1)} %collective-permute-done.6), channel_id=1, source_target_pairs={{0,1},{1,2},{2,3},{3,4},{4,5},{5,6},{6,7},{7,8},{8,9},{9,10},{10,1... | collective-permute-start | bytes 393224 | tf_op jit(solution)/shard_map/ppermute | solution.py:22
  44.7 6.9 %collective-permute-start.9 = (bf16[256,256]{1,0:T(8,128)(2,1)S(1)}, bf16[256,256]{1,0:T(8,128)(2,1)S(1)}, u32[]{:S(2)}, u32[]{:S(2)}) collective-permute-start(bf16[256,256]{1,0:T(8,128)(2,1)S(1)} %collective-permute-done.7), channel_id=1, source_target_pairs={{0,15},{1,0},{2,1},{3,2},{4,3},{5,4},{6,5},{7,6},{8,7},{9,8},{10,9... | collective-permute-start | bytes 393224 | tf_op jit(solution)/shard_map/ppermute | solution.py:25
  49.7 6.9 %collective-permute-start.10 = (bf16[256,256]{1,0:T(8,128)(2,1)S(1)}, bf16[256,256]{1,0:T(8,128)(2,1)S(1)}, u32[]{:S(2)}, u32[]{:S(2)}) collective-permute-start(bf16[256,256]{1,0:T(8,128)(2,1)S(1)} %collective-permute-done.8), channel_id=1, source_target_pairs={{0,1},{1,2},{2,3},{3,4},{4,5},{5,6},{6,7},{7,8},{8,9},{9,10},{10,1... | collective-permute-start | bytes 393224 | tf_op jit(solution)/shard_map/ppermute | solution.py:22
  51.6 6.9 %collective-permute-start.11 = (bf16[256,256]{1,0:T(8,128)(2,1)S(1)}, bf16[256,256]{1,0:T(8,128)(2,1)S(1)}, u32[]{:S(2)}, u32[]{:S(2)}) collective-permute-start(bf16[256,256]{1,0:T(8,128)(2,1)S(1)} %collective-permute-done.9), channel_id=1, source_target_pairs={{0,15},{1,0},{2,1},{3,2},{4,3},{5,4},{6,5},{7,6},{8,7},{9,8},{10,9... | collective-permute-start | bytes 393224 | tf_op jit(solution)/shard_map/ppermute | solution.py:25
  56.6 7.7 %collective-permute-start.12 = (bf16[256,256]{1,0:T(8,128)(2,1)S(1)}, bf16[256,256]{1,0:T(8,128)(2,1)S(1)}, u32[]{:S(2)}, u32[]{:S(2)}) collective-permute-start(bf16[256,256]{1,0:T(8,128)(2,1)S(1)} %collective-permute-done.10), channel_id=1, source_target_pairs={{0,1},{1,2},{2,3},{3,4},{4,5},{5,6},{6,7},{7,8},{8,9},{9,10},{10,1... | collective-permute-start | bytes 393224 | tf_op jit(solution)/shard_map/ppermute | solution.py:22
  58.5 7.7 %collective-permute-start.13 = (bf16[256,256]{1,0:T(8,128)(2,1)S(1)}, bf16[256,256]{1,0:T(8,128)(2,1)S(1)}, u32[]{:S(2)}, u32[]{:S(2)}) collective-permute-start(bf16[256,256]{1,0:T(8,128)(2,1)S(1)} %collective-permute-done.11), channel_id=1, source_target_pairs={{0,15},{1,0},{2,1},{3,2},{4,3},{5,4},{6,5},{7,6},{8,7},{9,8},{10,9... | collective-permute-start | bytes 393224 | tf_op jit(solution)/shard_map/ppermute | solution.py:25
  63.2 17.2 %copy-start.5 = (s32[1,32,8]{1,2,0:T(8,128)S(1)}, s32[1,32,8]{1,2,0:T(8,128)}, u32[]{:S(2)}) copy-start(s32[1,32,8]{1,2,0:T(8,128)} %param.15) | copy-start | bytes 3076
  63.2 17.2 %copy-start.6 = (s32[1,32,8]{1,2,0:T(8,128)S(1)}, s32[1,32,8]{1,2,0:T(8,128)}, u32[]{:S(2)}) copy-start(s32[1,32,8]{1,2,0:T(8,128)} %param.14) | copy-start | bytes 3076
  64.3 8.1 %collective-permute-start.14 = (bf16[256,256]{1,0:T(8,128)(2,1)S(1)}, bf16[256,256]{1,0:T(8,128)(2,1)S(1)}, u32[]{:S(2)}, u32[]{:S(2)}) collective-permute-start(bf16[256,256]{1,0:T(8,128)(2,1)S(1)} %collective-permute-done.12), channel_id=1, source_target_pairs={{0,1},{1,2},{2,3},{3,4},{4,5},{5,6},{6,7},{7,8},{8,9},{9,10},{10,1... | collective-permute-start | bytes 393224 | tf_op jit(solution)/shard_map/ppermute | solution.py:22
  66.3 21.7 %copy-start.1 = (f32[1,32,256]{2,1,0:T(8,128)S(1)}, f32[1,32,256]{2,1,0:T(8,128)}, u32[]{:S(2)}) copy-start(f32[1,32,256]{2,1,0:T(8,128)} %param.12) | copy-start | bytes 98308
  73.6 14.3 %all-to-all-start = ((bf16[16,32,256]{2,1,0:T(8,128)(2,1)}), bf16[16,32,256]{2,1,0:T(8,128)(2,1)S(1)}, u32[]{:S(2)}, u32[]{:S(2)}) async-start(bf16[16,32,256]{2,1,0:T(8,128)(2,1)} %bitcast.102), calls=%async_computation | async-start | bytes 524288 | tf_op jit(solution)/shard_map/all_to_all | solution.py:40
  80.3 117.8 %all-gather.4.cloned.1.call-start = ((), (), s32[]{:S(2)}) async-start(), calls=%async_computation.4 | async-start | bytes 3932160 | tf_op jit(solution)/shard_map/all_gather | solution.py:53
  103.3 94.9 %copy-start.7 = (bf16[1,192,4096]{2,1,0:T(8,128)(2,1)S(1)}, bf16[1,192,4096]{2,1,0:T(8,128)(2,1)}, u32[]{:S(2)}) copy-start(bf16[1,192,4096]{2,1,0:T(8,128)(2,1)} %param.17) | copy-start | bytes 4718596
  255.6 17.9 %copy-start.4 = (f32[1,32,8]{1,2,0:T(8,128)S(1)}, f32[1,32,8]{1,2,0:T(8,128)}, u32[]{:S(2)}) copy-start(f32[1,32,8]{1,2,0:T(8,128)} %param.16) | copy-start | bytes 3076
  259.0 36.0 %all-to-all-start.3 = ((bf16[32,12,256]{2,1,0:T(8,128)(2,1)}), bf16[32,12,256]{2,1,0:T(8,128)(2,1)S(1)}, u32[]{:S(2)}, u32[]{:S(2)}) async-start(bf16[32,12,256]{2,1,0:T(8,128)(2,1)} %copy.29), calls=%async_computation.3 | async-start | bytes 524288 | tf_op jit(solution)/shard_map/all_to_all | solution.py:99
Sparse Core Ops, SparseCore 0:
  161.4 36.7 all-gather.3
